TPU v7x, 32 devices: a whole 2x2x4 slice. The times are simulated.
32 devices in a mesh: tile: 16 (over z, y, x), chan: 2 (over core).
Axes of the slice: x: 2, y: 2, z: 4, core: 2. Of those that a mesh axis runs over, the one named last changes fastest.
Arguments:
- panels: bfloat16 [64, 2, 256, 256], P('tile', 'chan'), may hold values from -6 to 6
- pair_ends: int32 [128, 2], P('tile'), may hold values from 0 to 63, as said below
- peaks: int32 [128, 8, 2], P(('tile', 'chan')), may hold values from 0 to 255
Outputs:
- surface: bfloat16 [128, 256, 256], P(('tile', 'chan'))
- scores: float32 [128, 8], P(('tile', 'chan'))
Inputs may be any that keep to these rules, and one draw needn't show every extreme that they name: `pair_ends`: rows p * 8 to (p + 1) * 8 - 1 belong to tile index p: their column 0 is a tile of that index's block of 4 tiles, column 1 another tile whose block is at most 2 indices away; distances 2 and -2 both occur.
All inputs are finite; a program needn't handle non-finite values.
Results may differ from a plain program's by a relative error of at most 0.017.
Values may be sent and summed in bfloat16 or wider, within the bound.
No kernel may reach another device: no remote copies, remote signals or barrier semaphores. Data moves between devices by JAX's collectives and lax.ppermute only.
A program may use at most 64 MiB of HBM per device.

v0:
```python
import math

import jax
import jax.numpy as jnp
from jax import lax
from jax.sharding import PartitionSpec as P

REACH = 2


SIGMA = 0.5
FLOOR = 0.05


def shifted(value, axis, by):
    devices = lax.axis_size(axis)
    pairs = [(i, i + by) for i in range(devices) if 0 <= i + by < devices]
    return lax.ppermute(value, axis, pairs)


def fourier_tables(size):
    index = jnp.arange(size, dtype=jnp.int32)
    product = index[:, None] * index[None, :] % size
    angle = product.astype(jnp.float32) * (2.0 * math.pi / size)
    return (jnp.cos(angle).astype(jnp.bfloat16), jnp.sin(angle).astype(jnp.bfloat16))


def gauss_table(size):
    index = jnp.arange(size, dtype=jnp.float32)
    offset = index[:, None] - index[None, :]
    weight = jnp.exp(-offset * offset / (2.0 * SIGMA * SIGMA))
    return (weight / jnp.sum(weight, axis=1, keepdims=True)).astype(jnp.bfloat16)


def spectra(stack, gauss, cosine, sine):
    count = stack.shape[0]
    size = stack.shape[-1]
    both_tables = jnp.concatenate([cosine, sine], axis=1)
    first = jnp.dot(stack.reshape(count * size, size), gauss.T, preferred_element_type=jnp.float32)
    first = first.astype(jnp.bfloat16).reshape(count, size, size)
    smooth = jnp.einsum("kn,bnm->bkm", gauss, first, preferred_element_type=jnp.float32).astype(
        jnp.bfloat16
    )
    rotated = jnp.dot(
        smooth.reshape(count * size, size), both_tables, preferred_element_type=jnp.float32
    )
    rotated = rotated.reshape(count, size, 2 * size)
    part_real = rotated[:, :, :size].astype(jnp.bfloat16)
    part_imag = (-rotated[:, :, size:]).astype(jnp.bfloat16)
    spec_real = (
        jnp.einsum("kn,bnm->bkm", cosine, part_real, preferred_element_type=jnp.float32)
        + jnp.einsum("kn,bnm->bkm", sine, part_imag, preferred_element_type=jnp.float32)
    ) / size
    spec_imag = (
        jnp.einsum("kn,bnm->bkm", cosine, part_imag, preferred_element_type=jnp.float32)
        - jnp.einsum("kn,bnm->bkm", sine, part_real, preferred_element_type=jnp.float32)
    ) / size
    return (spec_real, spec_imag)


def shards(panels, pair_ends, peaks):
    tile_dev = panels.shape[0]
    size = panels.shape[-1]
    here = lax.axis_index("tile")
    local = panels[:, 0]
    cosine, sine = fourier_tables(size)
    gauss = gauss_table(size)
    blocks = []
    for offset in range(-REACH, REACH + 1):
        if offset == 0:
            blocks.append(local)
        else:
            blocks.append(shifted(local, "tile", -offset))
    real_all, imag_all = spectra(jnp.concatenate(blocks, axis=0), gauss, cosine, sine)
    first_tile = pair_ends[:, 0]
    second_tile = pair_ends[:, 1]
    row_first = first_tile - here * tile_dev + REACH * tile_dev
    row_second = (second_tile // tile_dev - here + REACH) * tile_dev + second_tile % tile_dev
    real_a = real_all[row_first]
    imag_a = imag_all[row_first]
    real_b = real_all[row_second]
    imag_b = imag_all[row_second]
    cross_real = real_a * real_b + imag_a * imag_b
    cross_imag = imag_a * real_b - real_a * imag_b
    share = pair_ends.shape[0] // lax.axis_size("chan")
    total_real, total_imag = (
        lax.psum(cross_real.astype(jnp.bfloat16), "chan").astype(jnp.float32),
        lax.psum(cross_imag.astype(jnp.bfloat16), "chan").astype(jnp.float32),
    )
    start = lax.axis_index("chan") * share
    cross_real = lax.dynamic_slice_in_dim(total_real, start, share, 0)
    cross_imag = lax.dynamic_slice_in_dim(total_imag, start, share, 0)
    magnitude = jnp.sqrt(cross_real * cross_real + cross_imag * cross_imag)
    level = jnp.mean(magnitude, axis=(1, 2), keepdims=True) + 1e-06
    denom = magnitude + FLOOR * level
    q_real = (cross_real / denom).astype(jnp.bfloat16)
    q_imag = (cross_imag / denom).astype(jnp.bfloat16)
    both_tables = jnp.concatenate([cosine, sine], axis=1)
    from_real = jnp.dot(
        q_real.reshape(share * size, size), both_tables, preferred_element_type=jnp.float32
    )
    from_imag = jnp.dot(
        q_imag.reshape(share * size, size), both_tables, preferred_element_type=jnp.float32
    )
    from_real = from_real.reshape(share, size, 2 * size)
    from_imag = from_imag.reshape(share, size, 2 * size)
    y_real = (from_real[:, :, :size] - from_imag[:, :, size:]).astype(jnp.bfloat16)
    y_imag = (from_real[:, :, size:] + from_imag[:, :, :size]).astype(jnp.bfloat16)
    corr = (
        jnp.einsum("kn,bnm->bkm", cosine, y_real, preferred_element_type=jnp.float32)
        - jnp.einsum("kn,bnm->bkm", sine, y_imag, preferred_element_type=jnp.float32)
    ) / size
    flat_index = peaks[:, :, 0] * size + peaks[:, :, 1]
    scores = jnp.take_along_axis(corr.reshape(share, size * size), flat_index, axis=1)
    return (corr.astype(jnp.bfloat16), scores)


def solution(mesh):
    in_specs = (P("tile", "chan", None, None), P("tile", None), P(("tile", "chan"), None, None))
    out_specs = (P(("tile", "chan"), None, None), P(("tile", "chan"), None))
    return jax.shard_map(shards, mesh=mesh, in_specs=in_specs, out_specs=out_specs, check_vma=False)
```

profile of v0, /device:TPU:0, one launch (start us, length us, event | category | flops | bytes accessed | tf_op | source)
XLA Modules:
  0.0 140.3 jit_solution(3158174900433382977)
XLA Ops:
  7.2 0.0 copy-start.1
  7.2 0.0 all-reduce.3.cloned.1.call-start
  7.2 5.0 %collective-permute-start = (bf16[4,256,256]{2,1,0:T(8,128)(2,1)}, bf16[4,256,256]{2,1,0:T(8,128)(2,1)S(1)}, u32[]{:S(2)}, u32[]{:S(2)}) collective-permute-start(bf16[4,256,256]{2,1,0:T(8,128)(2,1)} %bitcast.52), channel_id=1, source_target_pairs={{0,4},{2,6},{4,8},{6,10},{8,12},{10,14},{12,16},{14,18},{16,20},{1... | collective-permute-start | bytes 1572872 | tf_op jit(solution)/shard_map/ppermute | solution.py:18
  12.3 3.4 %collective-permute-start.1 = (bf16[4,256,256]{2,1,0:T(8,128)(2,1)}, bf16[4,256,256]{2,1,0:T(8,128)(2,1)S(1)}, u32[]{:S(2)}, u32[]{:S(2)}) collective-permute-start(bf16[4,256,256]{2,1,0:T(8,128)(2,1)} %bitcast.53), channel_id=1, source_target_pairs={{0,2},{2,4},{4,6},{6,8},{8,10},{10,12},{12,14},{14,16},{16,18},{18... | collective-permute-start | bytes 1572872 | tf_op jit(solution)/shard_map/ppermute | solution.py:18
  15.7 1.3 collective-permute-start.2
  17.0 1.3 collective-permute-start.3
  18.3 1.1 sine_convert_fusion
  19.4 0.8 fusion.51
  20.2 0.2 fusion.39
  20.4 14.6 %collective-permute-done = bf16[4,256,256]{2,1,0:T(8,128)(2,1)S(1)} collective-permute-done((bf16[4,256,256]{2,1,0:T(8,128)(2,1)}, bf16[4,256,256]{2,1,0:T(8,128)(2,1)S(1)}, u32[]{:S(2)}, u32[]{:S(2)}) %collective-permute-start) | collective-permute-done | bytes 524320 | tf_op jit(solution)/shard_map/ppermute | solution.py:18
  35.0 1.3 collective-permute-done.1
  36.4 0.0 copy-done.1
  36.4 3.5 %collective-permute-done.2 = bf16[4,256,256]{2,1,0:T(8,128)(2,1)S(1)} collective-permute-done((bf16[4,256,256]{2,1,0:T(8,128)(2,1)}, bf16[4,256,256]{2,1,0:T(8,128)(2,1)S(1)}, u32[]{:S(2)}, u32[]{:S(2)}) %collective-permute-start.2) | collective-permute-done | bytes 524320 | tf_op jit(solution)/shard_map/ppermute | solution.py:18
  40.0 0.0 collective-permute-done.3
  40.1 0.9 convolution_convert_fusion
  41.0 7.8 %fusion.1 = f32[20,256,512]{2,1,0:T(8,128)} fusion(bf16[20,256,256]{2,1,0:T(8,128)(2,1)S(1)} %bitcast.48, f32[256]{0:T(256)S(1)} %fusion.39, bf16[256,256]{1,0:T(8,128)(2,1)S(1)} %get-tuple-element.18, bf16[256,256]{1,0:T(8,128)(2,1)S(1)} %get-tuple-element.19), kind=kOutput, calls=%fused_computation.11 | convolution fusion | flops 2015494144 | bytes 13370368 | tf_op jit(solution)/shard_map/dot_general | solution.py:44
  48.8 0.0 copy-start
  48.9 4.4 %fusion.14 = f32[20,256,256]{2,1,0:T(8,128)S(1)} fusion(f32[20,256,512]{2,1,0:T(8,128)} %fusion.1), kind=kOutput, calls=%fused_computation.32 | convolution fusion | flops 672071680 | bytes 7864320 | tf_op jit(solution)/shard_map/kn,bnm->bkm/dot_general | solution.py:51
  53.3 1.1 copy-done
  54.4 4.2 %fusion.16 = f32[20,256,256]{2,1,0:T(8,128)} fusion(f32[20,256,512]{2,1,0:T(8,128)S(1)} %copy-done), kind=kOutput, calls=%fused_computation.34 | convolution fusion | flops 674693120 | bytes 10485760 | tf_op jit(solution)/shard_map/kn,bnm->bkm/dot_general | solution.py:55
  58.6 4.1 %multiply_bitcast_fusion.1 = f32[20,256,256]{1,2,0:T(8,128)} fusion(f32[20,256,256]{2,1,0:T(8,128)S(1)} %fusion.14, f32[20,256,512]{2,1,0:T(8,128)S(1)} %copy-done), kind=kOutput, calls=%fused_computation.10 | convolution fusion | flops 677314560 | bytes 15728640 | tf_op jit(solution)/shard_map/kn,bnm->bkm/dot_general | solution.py:52
  62.7 3.2 %gather_fusion.1 = f32[8,256,256]{1,2,0:T(8,128)S(1)} fusion(f32[20,256,256]{1,2,0:T(8,128)} %multiply_bitcast_fusion.1, s32[1024]{0:T(1024)S(1)} %get-tuple-element.20), kind=kCustom, calls=%fused_computation.1 | custom fusion | bytes 4194336 | tf_op jit(solution)/shard_map/gather | solution.py:81
  65.9 4.5 %gather_fusion = f32[8,256,256]{1,2,0:T(8,128)} fusion(f32[20,256,256]{1,2,0:T(8,128)} %multiply_bitcast_fusion.1, s32[1024]{0:T(1024)S(1)} %get-tuple-element.21), kind=kCustom, calls=%fused_computation | custom fusion | bytes 4194336 | tf_op jit(solution)/shard_map/gather | solution.py:79
  70.4 8.4 %multiply_bitcast_fusion = f32[20,256,256]{1,2,0:T(8,128)} fusion(f32[20,256,256]{2,1,0:T(8,128)} %fusion.16, f32[20,256,512]{2,1,0:T(8,128)} %fusion.1), kind=kOutput, calls=%fused_computation.9 | convolution fusion | flops 674693120 | bytes 13107200 | tf_op jit(solution)/shard_map/kn,bnm->bkm/dot_general | solution.py:56
  78.8 4.5 %gather_fusion.3 = f32[8,256,256]{1,2,0:T(8,128)} fusion(f32[20,256,256]{1,2,0:T(8,128)} %multiply_bitcast_fusion, s32[1024]{0:T(1024)S(1)} %get-tuple-element.20), kind=kCustom, calls=%fused_computation.3 | custom fusion | bytes 4194336 | tf_op jit(solution)/shard_map/gather | solution.py:82
  83.3 4.5 %gather_fusion.2 = f32[8,256,256]{1,2,0:T(8,128)} fusion(f32[20,256,256]{1,2,0:T(8,128)} %multiply_bitcast_fusion, s32[1024]{0:T(1024)S(1)} %get-tuple-element.21), kind=kCustom, calls=%fused_computation.2 | custom fusion | bytes 4194336 | tf_op jit(solution)/shard_map/gather | solution.py:80
  87.8 0.0 copy-start.4
  87.8 4.9 %add_convert_fusion = (bf16[8,256,256]{1,2,0:T(8,128)(2,1)}, bf16[8,256,256]{1,2,0:T(8,128)(2,1)}) fusion(f32[8,256,256]{1,2,0:T(8,128)} %gather_fusion.2, f32[8,256,256]{1,2,0:T(8,128)} %gather_fusion.3, f32[8,256,256]{1,2,0:T(8,128)} %gather_fusion, f32[8,256,256]{1,2,0:T(8,128)S(1)} %gather_fusion.1), kind=kLoop, calls=%fused_computation.16 | loop fusion | flops 4194304 | bytes 10485760 | tf_op jit(solution)/shard_map/convert_element_type | solution.py:87
  92.7 0.0 all-reduce.3.cloned.1.call-update
  92.7 0.0 copy-done.4
  92.8 0.1 reshape.75
  92.9 29.9 %all-reduce.3.cloned.1.call-done = (bf16[8,256,256]{1,2,0:T(8,128)(2,1)}, bf16[8,256,256]{1,2,0:T(8,128)(2,1)}) async-done(((bf16[8,256,256]{1,2,0:T(8,128)(2,1)}, bf16[8,256,256]{1,2,0:T(8,128)(2,1)}), (bf16[8,256,256]{1,2,0:T(8,128)(2,1)}, bf16[8,256,256]{1,2,0:T(8,128)(2,1)})) %all-reduce.3.cloned.1.call-update) | async-done | bytes 2097168 | tf_op jit(solution)/shard_map/psum | solution.py:88
  122.7 1.7 %fusion.15 = f32[4]{0:T(128)S(1)} fusion(bf16[8,256,256]{1,2,0:T(8,128)(2,1)} %get-tuple-element.8, s32[]{:T(128)S(6)} %select_n.63, bf16[8,256,256]{1,2,0:T(8,128)(2,1)} %get-tuple-element.9), kind=kLoop, calls=%fused_computation.33 | loop fusion | flops 1572860 | bytes 1048596 | tf_op jit(solution)/shard_map/reduce_sum | solution.py:94
  124.5 0.0 copy-start.2
  124.5 0.0 copy-start.3
  124.5 2.1 %fusion.21 = f32[4,256,512]{2,1,0:T(8,128)S(1)} fusion(f32[4]{0:T(128)S(1)} %add_multiply_fusion, bf16[8,256,256]{1,2,0:T(8,128)(2,1)} %get-tuple-element.8, s32[]{:T(128)S(6)} %select_n.63, bf16[8,256,256]{1,2,0:T(8,128)(2,1)} %get-tuple-element.9, bf16[256,256]{1,0:T(8,128)(2,1)S(1)} %get-tuple-element.18, bf16[256,256]{1,0:T(8,128)(2,1)S(1)} %get-tuple-element.19), kind=kOutput, calls=%fused_computation.36 | convolution fusion | flops 271056896 | bytes 3407892 | tf_op jit(solution)/shard_map/dot_general | solution.py:99
  126.6 0.0 copy-done.2
  126.6 0.0 copy-done.3
  126.6 0.8 fusion.19
  127.4 1.3 fusion.23
  128.7 1.3 fusion.84
  130.0 0.3 copy.34
  130.3 0.7 copy.47
  131.0 0.8 gather_fusion.4
  131.8 0.1 reshape.78
  131.9 1.0 copy.35
  132.9 0.6 bitcast_select_fusion
  (9 shorter events, 0.2 us)
Async XLA Ops:
  7.2 29.2 %copy-start.1 = (bf16[4,1,256,256]{3,2,1,0:T(8,128)(2,1)S(1)}, bf16[4,1,256,256]{3,2,1,0:T(8,128)(2,1)}, u32[]{:S(2)}) copy-start(bf16[4,1,256,256]{3,2,1,0:T(8,128)(2,1)} %param.3) | copy-start | bytes 1572868
  7.2 115.6 %all-reduce.3.cloned.1.call-start = ((), (), s32[]{:S(2)}) async-start(), calls=%async_computation | async-start | bytes 4194304 | tf_op jit(solution)/shard_map/psum | solution.py:88
  7.2 27.7 %collective-permute-start = (bf16[4,256,256]{2,1,0:T(8,128)(2,1)}, bf16[4,256,256]{2,1,0:T(8,128)(2,1)S(1)}, u32[]{:S(2)}, u32[]{:S(2)}) collective-permute-start(bf16[4,256,256]{2,1,0:T(8,128)(2,1)} %bitcast.52), channel_id=1, source_target_pairs={{0,4},{2,6},{4,8},{6,10},{8,12},{10,14},{12,16},{14,18},{16,20},{1... | collective-permute-start | bytes 1572872 | tf_op jit(solution)/shard_map/ppermute | solution.py:18
  12.3 24.1 %collective-permute-start.1 = (bf16[4,256,256]{2,1,0:T(8,128)(2,1)}, bf16[4,256,256]{2,1,0:T(8,128)(2,1)S(1)}, u32[]{:S(2)}, u32[]{:S(2)}) collective-permute-start(bf16[4,256,256]{2,1,0:T(8,128)(2,1)} %bitcast.53), channel_id=1, source_target_pairs={{0,2},{2,4},{4,6},{6,8},{8,10},{10,12},{12,14},{14,16},{16,18},{18... | collective-permute-start | bytes 1572872 | tf_op jit(solution)/shard_map/ppermute | solution.py:18
  15.7 24.3 %collective-permute-start.2 = (bf16[4,256,256]{2,1,0:T(8,128)(2,1)}, bf16[4,256,256]{2,1,0:T(8,128)(2,1)S(1)}, u32[]{:S(2)}, u32[]{:S(2)}) collective-permute-start(bf16[4,256,256]{2,1,0:T(8,128)(2,1)} %bitcast.54), channel_id=1, source_target_pairs={{2,0},{4,2},{6,4},{8,6},{10,8},{12,10},{14,12},{16,14},{18,16},{20... | collective-permute-start | bytes 1572872 | tf_op jit(solution)/shard_map/ppermute | solution.py:18
  17.0 23.0 %collective-permute-start.3 = (bf16[4,256,256]{2,1,0:T(8,128)(2,1)}, bf16[4,256,256]{2,1,0:T(8,128)(2,1)S(1)}, u32[]{:S(2)}, u32[]{:S(2)}) collective-permute-start(bf16[4,256,256]{2,1,0:T(8,128)(2,1)} %bitcast.55), channel_id=1, source_target_pairs={{4,0},{6,2},{8,4},{10,6},{12,8},{14,10},{16,12},{18,14},{20,16},{2... | collective-permute-start | bytes 1572872 | tf_op jit(solution)/shard_map/ppermute | solution.py:18
  48.8 5.5 %copy-start = (f32[20,256,512]{2,1,0:T(8,128)S(1)}, f32[20,256,512]{2,1,0:T(8,128)}, u32[]{:S(2)}) copy-start(f32[20,256,512]{2,1,0:T(8,128)} %fusion.1) | copy-start | bytes 31457284
  87.8 5.0 %copy-start.4 = (s32[4,8,2]{1,2,0:T(2,128)S(1)}, s32[4,8,2]{1,2,0:T(2,128)}, u32[]{:S(2)}) copy-start(s32[4,8,2]{1,2,0:T(2,128)} %param.5) | copy-start | bytes 772
  124.5 2.1 %copy-start.2 = (bf16[8,256,256]{1,2,0:T(8,128)(2,1)S(1)}, bf16[8,256,256]{1,2,0:T(8,128)(2,1)}, u32[]{:S(2)}) copy-start(bf16[8,256,256]{1,2,0:T(8,128)(2,1)} %get-tuple-element.8) | copy-start | bytes 3145732
  124.5 2.1 %copy-start.3 = (bf16[8,256,256]{1,2,0:T(8,128)(2,1)S(1)}, bf16[8,256,256]{1,2,0:T(8,128)(2,1)}, u32[]{:S(2)}) copy-start(bf16[8,256,256]{1,2,0:T(8,128)(2,1)} %get-tuple-element.9) | copy-start | bytes 3145732
Sparse Core Ops, SparseCore 0:
  92.8 29.8 all-reduce.2
where the time goes:
time: 141 us; the launch traced here: 140 us
  waiting for transfers between devices  49.3 us (35%)
  matrix products  35.5 us (25%)
  local copies, waits for them, and re-layouts  20.8 us (15%)
  between operations  14.2 us (10%)
  starting transfers between devices  11.1 us (8%)
  other arithmetic  9.36 us (7%)
    psum x1, waiting for transfers between devices, shards(): lax.psum(cross_imag.astype(jnp.bfloat16), 'chan').astype(jnp.float32)  29.9 us
    ppermute x4, waiting for transfers between devices, shifted(): return lax.ppermute(value, axis, pairs)  19.5 us
    ppermute x4, starting transfers between devices, shifted(): return lax.ppermute(value, axis, pairs)  11 us
    dot_general x1, matrix products, spectra(): jnp.einsum('kn,bnm->bkm', sine, part_real, preferred_element_type=jnp.flo...  8.45 us
    dot_general x1, matrix products, spectra(): jnp.dot(smooth.reshape(count * size, size), both_tables, preferred_elemen...  7.84 us
    convert_element_type x1, other arithmetic, shards(): cross_real.astype(jnp.bfloat16)  4.94 us
    gather x1, local copies, waits for them, and re-layouts, shards(): imag_b = imag_all[row_second]  4.49 us
    gather x1, local copies, waits for them, and re-layouts, shards(): real_a = real_all[row_first]  4.49 us
  transfers between devices with their start and end apart: 5, of which 4 were waited for; matrix products, arithmetic and copies ran while one was open for 2% of the time, Pallas kernels for 0%

commit v1 on v0

v1 whole, which is shorter than its diff:
```python
import functools
import math

import jax
import jax.numpy as jnp
import ml_dtypes
import numpy as np
from jax import lax
from jax.experimental import pallas as pl
from jax.experimental.pallas import tpu as pltpu
from jax.sharding import PartitionSpec as P

SIGMA = 0.5
FLOOR = 0.05
PLANE = 4
EXTRA = 16
BOTH = ("tile", "chan")
VMEM = pl.BlockSpec(memory_space=pltpu.VMEM)
SMEM = pl.BlockSpec(memory_space=pltpu.SMEM)
ANY = pl.BlockSpec(memory_space=pl.ANY)


def tables(size):
    index = np.arange(size)
    angle = (index[:, None] * index[None, :] % size) * (2.0 * math.pi / size)
    cosine = np.cos(angle).astype(ml_dtypes.bfloat16).astype(np.float64)
    sine = np.sin(angle).astype(ml_dtypes.bfloat16).astype(np.float64)
    offset = index[:, None] - index[None, :]
    weight = np.exp(-offset * offset / (2.0 * SIGMA * SIGMA))
    gauss = weight / weight.sum(axis=1, keepdims=True)
    half = size // 2
    columns = np.concatenate([cosine, -sine], axis=1)
    pad = np.zeros((EXTRA - 1, 2 * size))
    real = np.concatenate([cosine, sine], axis=1) / size
    imag = np.concatenate([-sine, cosine], axis=1) / size
    rows = np.concatenate([real[:half], imag[:half], real[half : half + 1], pad, imag[half : half + 1], pad], axis=0)
    back = np.block([[cosine, sine], [-sine, cosine]])
    twice = np.full((1, half), 2.0)
    twice[0, 0] = 1.0
    sines = -sine[:, :half] * twice
    sines[:, 0] = cosine[:, half]
    last = np.concatenate([cosine[:, :half] * twice, sines], axis=1) / size
    return [jnp.asarray(t.astype(ml_dtypes.bfloat16)) for t in (gauss.T, gauss, columns, rows, back, last)]


def product(left, right):
    return jnp.dot(left, right, preferred_element_type=jnp.float32)


def spectrum(panel, gauss_t, gauss, columns, rows):
    size = panel.shape[-1]
    first = product(panel, gauss_t[...]).astype(jnp.bfloat16)
    smooth = product(gauss[...], first).astype(jnp.bfloat16)
    part = product(smooth, columns[...]).astype(jnp.bfloat16)
    return product(rows[...], jnp.concatenate([part[:, :size], part[:, size:]], axis=0))


def local_kernel(panels, gauss_t, gauss, columns, rows, out):
    for tile in range(panels.shape[0]):
        out[tile] = spectrum(panels[tile], gauss_t, gauss, columns, rows)


def split(slab, half):
    return (slab[:half], slab[half : 2 * half], slab[2 * half : 2 * half + EXTRA], slab[2 * half + EXTRA :])


def cross_kernel(mine, ends, panels, *refs):
    blocks, (spectra, gauss_t, gauss, columns, rows, out, taken, sems) = refs[:5], refs[5:]
    here = lax.axis_index("tile")
    chan = lax.axis_index("chan")
    tile_dev = panels.shape[0]
    half = panels.shape[-1] // 2
    count = out.shape[0]
    first_pair = count * (chan if mine else 1 - chan)
    place = here % PLANE
    outer = (place == 0) | (place == 3)
    one = jnp.where(place % 2 == 0, 1, -1)
    two = jnp.where(place < 2, 2, -2)
    copies = []
    for k in range(count):
        tile = ends[2 * (first_pair + k) + 1]
        away = tile // tile_dev - here
        slot = tile % tile_dev
        even = chan == 0
        by_x = away == one
        by_y = away == two
        by_z = away == -two
        by_d = away == -one
        picks = [
            (away == 0, panels),
            ((by_y & even) | (by_x & ~even), blocks[0]),
            ((by_x & even) | (by_y & ~even), blocks[1]),
            (by_z & even, blocks[2]),
            (by_d, blocks[3]),
            (by_z & ~even, blocks[4]),
        ]
        for pick, source in picks:

            @pl.when(pick)
            def _(source=source):
                pltpu.make_async_copy(source.at[slot], taken.at[k], sems.at[k]).start()

    for k in range(count):
        pltpu.make_async_copy(panels.at[0], taken.at[k], sems.at[k]).wait()
        b_real, b_imag, b_real_x, b_imag_x = split(spectrum(taken[k], gauss_t, gauss, columns, rows), half)
        a = spectra.at[ends[2 * (first_pair + k)] - here * tile_dev]
        a_real, a_imag, a_real_x, a_imag_x = split(a[...], half)
        out[k] = jnp.concatenate(
            [
                a_real * b_real + a_imag * b_imag,
                a_imag * b_real - a_real * b_imag,
                a_real_x * b_real_x + a_imag_x * b_imag_x,
                a_imag_x * b_real_x - a_real_x * b_imag_x,
            ],
            axis=0,
        ).astype(jnp.bfloat16)


def surface_kernel(peaks, mine, other, peak_columns, back, last, surface, scores, corr):
    count, _, size = surface.shape
    cand = scores.shape[1]
    half = size // 2
    for k in range(count):
        slab = mine[k].astype(jnp.float32) + other[k].astype(jnp.float32)
        real, imag, real_x, imag_x = split(slab, half)
        magnitude = jnp.sqrt(real * real + imag * imag)
        magnitude_x = jnp.sqrt(real_x * real_x + imag_x * imag_x)
        total = 2.0 * jnp.sum(magnitude) - jnp.sum(magnitude[:1]) + jnp.sum(magnitude_x)
        level = total / (size * size) + 1e-06
        scale = 1.0 / (magnitude + FLOOR * level)
        scale_x = 1.0 / (magnitude_x + FLOOR * level)
        q_real = jnp.concatenate([real * scale, real_x * scale_x], axis=0)
        q_imag = jnp.concatenate([imag * scale, imag_x * scale_x], axis=0)
        q = jnp.concatenate([q_real, q_imag], axis=1).astype(jnp.bfloat16)
        y = product(q, back[...])
        y_real = y[:half, :size]
        y_imag = y[:half, size:]
        row = lax.broadcasted_iota(jnp.int32, y_imag.shape, 0)
        y_imag = jnp.where(row == 0, y[half : half + 1, :size], y_imag)
        both = jnp.concatenate([y_real, y_imag], axis=0).astype(jnp.bfloat16)
        result = product(last[...], both)
        corr[k] = result
        surface[k] = result.astype(jnp.bfloat16)
    lane = lax.broadcasted_iota(jnp.int32, (cand, size), 1)
    diagonal = lax.broadcasted_iota(jnp.int32, (cand, cand), 0) == lax.broadcasted_iota(jnp.int32, (cand, cand), 1)
    for k in range(count):
        picked = jnp.concatenate([corr[k, pl.ds(peaks[k * cand + j], 1), :] for j in range(cand)], axis=0)
        found = jnp.sum(jnp.where(lane == peak_columns[k], picked, 0.0), axis=1, keepdims=True)
        scores[k : k + 1, :] = jnp.sum(jnp.where(diagonal, found, 0.0), axis=0, keepdims=True)


def routes(devices):
    def up(t, c):
        return (t + PLANE, c) if t + PLANE < devices else (t, 1 - c)

    def down(t, c):
        return (t - PLANE, c) if t >= PLANE else (t, 1 - c)

    def across(c, core):
        return 2 if c == core else 1

    def pairs(step):
        return [(2 * t + c, 2 * d + e) for t in range(devices) for c in range(2) for d, e in [step(t, c)]]

    return (
        pairs(lambda t, c: (t ^ across(c, 0), c)),
        pairs(lambda t, c: (t ^ across(c, 1), c)),
        pairs(lambda t, c: (up if (t % PLANE < 2) == (c == 0) else down)(t, c)),
        pairs(lambda t, c: (t ^ across(c, 1), c)),
        pairs(lambda t, c: (up if (t % PLANE < 2) == (c == 1) else down)(t, c)),
    )


def after(value, earlier):
    return lax.optimization_barrier((value, earlier))[0]


def shards(panels, pair_ends, peaks):
    tile_dev, _, size, _ = panels.shape
    share, cand, _ = peaks.shape
    devices = lax.axis_size("tile")
    local = panels[:, 0]
    gauss_t, gauss, columns, rows, back, last = tables(size)
    slab = size + 2 * EXTRA
    place = lax.axis_index("tile") % PLANE
    outer = (place == 0) | (place == 3)
    swap, cross_swap, climb, relay, climb_late = routes(devices)
    move = functools.partial(lax.ppermute, axis_name=BOTH)
    got_swap = move(local, perm=swap)
    got_climb = move(got_swap, perm=climb)
    got_cross = move(after(local, got_swap), perm=cross_swap)
    got_relay = move(jnp.where(outer, got_swap, got_climb), perm=relay)
    got_late = move(got_cross, perm=climb_late)
    blocks = (got_swap, got_cross, got_climb, got_relay, got_late)
    ends = pair_ends.reshape(-1)
    spectra = pl.pallas_call(
        local_kernel,
        out_shape=jax.ShapeDtypeStruct((tile_dev, slab, size), jnp.float32),
        in_specs=[VMEM] * 5,
        out_specs=VMEM,
        compiler_params=pltpu.CompilerParams(vmem_limit_bytes=32 << 20),
        cost_estimate=pl.CostEstimate(flops=tile_dev * 12 * size**3, bytes_accessed=4 << 20, transcendentals=0),
        name="local_spectra",
    )(local, gauss_t, gauss, columns, rows)

    def cross(mine):
        return pl.pallas_call(
            functools.partial(cross_kernel, mine),
            out_shape=jax.ShapeDtypeStruct((share, slab, size), jnp.bfloat16),
            in_specs=[SMEM] + [ANY] * 6 + [VMEM] * 5,
            out_specs=VMEM,
            scratch_shapes=[pltpu.VMEM((share, size, size), jnp.bfloat16), pltpu.SemaphoreType.DMA((share,))],
            compiler_params=pltpu.CompilerParams(vmem_limit_bytes=32 << 20),
            cost_estimate=pl.CostEstimate(flops=share * 12 * size**3, bytes_accessed=4 << 20, transcendentals=0),
            name="cross_mine" if mine else "cross_other",
        )(ends, local, *blocks, spectra, gauss_t, gauss, columns, rows)

    given = cross(False)
    other = lax.ppermute(given, "chan", [(0, 1), (1, 0)])
    kept = cross(True)
    surface, scores = pl.pallas_call(
        surface_kernel,
        out_shape=(
            jax.ShapeDtypeStruct((share, size, size), jnp.bfloat16),
            jax.ShapeDtypeStruct((share, cand), jnp.float32),
        ),
        in_specs=[SMEM] + [VMEM] * 5,
        out_specs=(VMEM, VMEM),
        scratch_shapes=[pltpu.VMEM((share, size, size), jnp.float32)],
        compiler_params=pltpu.CompilerParams(vmem_limit_bytes=32 << 20),
        cost_estimate=pl.CostEstimate(flops=share * 12 * size**3, bytes_accessed=4 << 20, transcendentals=0),
        name="surface",
    )(peaks[:, :, 0].reshape(-1), kept, other, peaks[:, :, 1:], back, last)
    return (surface, scores)


def solution(mesh):
    in_specs = (P("tile", "chan", None, None), P("tile", None), P(BOTH, None, None))
    out_specs = (P(BOTH, None, None), P(BOTH, None))
    return jax.shard_map(shards, mesh=mesh, in_specs=in_specs, out_specs=out_specs, check_vma=False)
```

time: 141 us -> 51.4 us (0.36)
  matrix products: 35.5 us -> 0 us
  waiting for transfers between devices: 49.3 us -> 17.4 us
  Pallas kernels: 0 us -> 15.5 us
  between operations: 14.2 us -> 0.76 us
  local copies, waits for them, and re-layouts: 20.8 us -> 8.32 us
  other arithmetic: 9.36 us -> 0.85 us
  starting transfers between devices: 11.1 us -> 8.17 us
    dot_general x10 -> x0, matrix products: 35.5 us -> none  [the longest x1 8.45 us: spectra(): jnp.einsum('kn,bnm->bkm', sine, part_real, preferred_element_type=jnp.flo...]
    psum x1 -> x0, waiting for transfers between devices: 29.9 us -> none  [shards(): lax.psum(cross_imag.astype(jnp.bfloat16), 'chan').astype(jnp.float32)]
    gather x7 -> x0, local copies, waits for them, and re-layouts: 17.5 us -> none  [the longest x1 4.49 us: shards(): imag_b = imag_all[row_second]]
    pallas_call x0 -> x4, Pallas kernels: none -> 15.5 us  [the longest x2 10.1 us: cross(): pl.pallas_call(functools.partial(cross_kernel, mine), out_shape=jax.Shape...]
    convert_element_type x2 -> x0, other arithmetic: 6.03 us -> none  [the longest x1 4.94 us: shards(): cross_real.astype(jnp.bfloat16)]
    unnamed x16 -> x32, local copies, waits for them, and re-layouts: 2.93 us -> 7.06 us
    ppermute x4 -> x6, starting transfers between devices: 11 us -> 8.17 us  [the longest x1 3.03 us: shards(): got_swap = move(local, perm=swap)]
    ppermute x4 -> x6, waiting for transfers between devices: 19.5 us -> 17.4 us  [the longest x1 7.37 us: shards(): got_swap = move(local, perm=swap)]
  transfers between devices with their start and end apart: 5 -> 6, of which waited for: 4 -> 5; matrix products, arithmetic and copies ran while one was open for 2% -> 6% of each run, Pallas kernels for 0% -> 13%
where the time goes in v1:
time: 51.4 us; the launch traced here: 51 us
  waiting for transfers between devices  17.4 us (34%)
  Pallas kernels  15.5 us (30%)
  local copies, waits for them, and re-layouts  8.32 us (16%)
  starting transfers between devices  8.17 us (16%)
  other arithmetic  0.85 us (2%)
  between operations  0.76 us (1%)
    pallas_call x2, Pallas kernels, cross(): pl.pallas_call(functools.partial(cross_kernel, mine), out_shape=jax.Shape...  10.1 us
    ppermute x1, waiting for transfers between devices, shards(): got_swap = move(local, perm=swap)  7.37 us
    unnamed x32, local copies, waits for them, and re-layouts  7.06 us
    ppermute x1, waiting for transfers between devices, shards(): got_climb = move(got_swap, perm=climb)  5.21 us
    pallas_call x1, Pallas kernels, shards(): pl.pallas_call(surface_kernel, out_shape=(jax.ShapeDtypeStruct((share, si...  3.43 us
    ppermute x1, starting transfers between devices, shards(): got_swap = move(local, perm=swap)  3.03 us
    ppermute x1, waiting for transfers between devices, shards(): got_relay = move(jnp.where(outer, got_swap, got_climb), perm=relay)  2.7 us
    ppermute x1, starting transfers between devices, shards(): got_climb = move(got_swap, perm=climb)  2.08 us
  transfers between devices with their start and end apart: 6, of which 5 were waited for; matrix products, arithmetic and copies ran while one was open for 6% of the time, Pallas kernels for 13%

profile of v1, /device:TPU:0, one launch (start us, length us, event | category | flops | bytes accessed | tf_op | source)
XLA Modules:
  0.0 51.0 jit_solution(8518966216297873726)
XLA Ops:
  0.6 0.0 copy-start.3
  0.6 0.0 copy-start
  0.7 0.0 copy-start.14
  0.7 3.0 %collective-permute-start = (bf16[4,256,256]{2,1,0:T(8,128)(2,1)}, bf16[4,256,256]{2,1,0:T(8,128)(2,1)S(1)}, u32[]{:S(2)}, u32[]{:S(2)}) collective-permute-start(bf16[4,256,256]{2,1,0:T(8,128)(2,1)} %bitcast.1), channel_id=1, source_target_pairs={{0,4},{1,3},{2,6},{3,1},{4,0},{5,7},{6,2},{7,5},{8,12},{9,11},{10,... | collective-permute-start | bytes 1572872 | tf_op jit(solution)/shard_map/ppermute | solution.py:189
  3.7 7.4 %collective-permute-done.refs_0_ = bf16[4,256,256]{2,1,0:T(8,128)(2,1)S(1)} collective-permute-done((bf16[4,256,256]{2,1,0:T(8,128)(2,1)}, bf16[4,256,256]{2,1,0:T(8,128)(2,1)S(1)}, u32[]{:S(2)}, u32[]{:S(2)}) %collective-permute-start) | collective-permute-done | bytes 524320 | tf_op jit(solution)/shard_map/ppermute | solution.py:189
  11.1 2.1 %collective-permute-start.2 = (bf16[4,256,256]{2,1,0:T(8,128)(2,1)S(1)}, bf16[4,256,256]{2,1,0:T(8,128)(2,1)S(1)}, u32[]{:S(2)}, u32[]{:S(2)}) collective-permute-start(bf16[4,256,256]{2,1,0:T(8,128)(2,1)S(1)} %collective-permute-done.refs_0_), channel_id=1, source_target_pairs={{0,8},{1,0},{2,10},{3,2},{4,5},{5,13},{6,7},{7,15},{8,16},{9,1},{1... | collective-permute-start | bytes 1572872 | tf_op jit(solution)/shard_map/ppermute | solution.py:190
  13.1 1.5 %collective-permute-start.1 = (bf16[4,256,256]{2,1,0:T(8,128)(2,1)}, bf16[4,256,256]{2,1,0:T(8,128)(2,1)S(1)}, u32[]{:S(2)}, u32[]{:S(2)}) collective-permute-start(bf16[4,256,256]{2,1,0:T(8,128)(2,1)} %bitcast.2), channel_id=1, source_target_pairs={{0,2},{1,5},{2,0},{3,7},{4,6},{5,1},{6,4},{7,3},{8,10},{9,13},{10,... | collective-permute-start | bytes 1572872 | tf_op jit(solution)/shard_map/ppermute | solution.py:191
  14.6 5.2 %collective-permute-done.2.refs_2_ = bf16[4,256,256]{2,1,0:T(8,128)(2,1)S(1)} collective-permute-done((bf16[4,256,256]{2,1,0:T(8,128)(2,1)S(1)}, bf16[4,256,256]{2,1,0:T(8,128)(2,1)S(1)}, u32[]{:S(2)}, u32[]{:S(2)}) %collective-permute-start.2) | collective-permute-done | bytes 524320 | tf_op jit(solution)/shard_map/ppermute | solution.py:190
  19.8 0.8 %broadcast_select_fusion = bf16[4,256,256]{2,1,0:T(8,128)(2,1)} fusion(bf16[4,256,256]{2,1,0:T(8,128)(2,1)S(1)} %collective-permute-done.refs_0_, bf16[4,256,256]{2,1,0:T(8,128)(2,1)S(1)} %collective-permute-done.2.refs_2_, pred[]{:T(512)S(6)} %or.3), kind=kLoop, calls=%fused_computation | loop fusion | flops 262144 | bytes 1572865 | tf_op jit(solution)/shard_map/jit(_where)/select_n | solution.py:192
  20.7 1.5 %collective-permute-start.3 = (bf16[4,256,256]{2,1,0:T(8,128)(2,1)}, bf16[4,256,256]{2,1,0:T(8,128)(2,1)}, u32[]{:S(2)}, u32[]{:S(2)}) collective-permute-start(bf16[4,256,256]{2,1,0:T(8,128)(2,1)} %broadcast_select_fusion), channel_id=1, source_target_pairs={{0,2},{1,5},{2,0},{3,7},{4,6},{5,1},{6,4},{7,3},{8,10},{9,13},{10,... | collective-permute-start | bytes 1572872 | tf_op jit(solution)/shard_map/ppermute | solution.py:192
  22.2 0.4 collective-permute-done.1.refs_1_
  22.5 0.0 collective-permute-start.4
  22.5 0.0 copy-done.14
  22.5 0.1 copy.13
  22.6 0.1 reshape.7.ends
  22.7 0.0 copy-done.3
  22.7 0.0 copy-done
  22.7 0.0 copy-start.1
  22.7 1.0 %copy-done.1 = bf16[288,512]{1,0:T(8,128)(2,1)S(1)} copy-done((bf16[288,512]{1,0:T(8,128)(2,1)S(1)}, bf16[288,512]{1,0:T(8,128)(2,1)}, u32[]{:S(2)}) %copy-start.1) | copy-done | bytes 294936
  23.7 0.0 copy-start.4
  23.7 0.9 %copy-done.4 = bf16[256,256]{1,0:T(8,128)(2,1)S(1)} copy-done((bf16[256,256]{1,0:T(8,128)(2,1)S(1)}, bf16[256,256]{1,0:T(8,128)(2,1)}, u32[]{:S(2)}) %copy-start.4) | copy-done | bytes 131096
  24.6 0.0 copy-start.6
  24.6 0.9 %copy-done.6 = bf16[256,256]{1,0:T(8,128)(2,1)S(1)} copy-done((bf16[256,256]{1,0:T(8,128)(2,1)S(1)}, bf16[256,256]{1,0:T(8,128)(2,1)}, u32[]{:S(2)}) %copy-start.6) | copy-done | bytes 131096
  25.5 0.0 copy-start.8
  25.5 2.0 %local_spectra.1.refs_5_ = f32[4,288,256]{2,1,0:T(8,128)S(1)} custom-call(bf16[4,256,256]{2,1,0:T(8,128)(2,1)S(1)} %bitcast.3, bf16[256,256]{1,0:T(8,128)(2,1)S(1)} %copy-done.4, bf16[256,256]{1,0:T(8,128)(2,1)S(1)} %copy-done.6, bf16[256,512]{1,0:T(8,128)(2,1)S(1)} %copy-done.3, bf16[288,512]{1,0:T(8,128)(2,1)S(1)} %copy-done.1), custom_call_target="tpu_custom_call" | custom-call | flops 805306368 | bytes 4194304 | tf_op jit(solution)/shard_map/local_spectra/pallas_call | solution.py:196
  27.5 0.0 copy-start.13
  27.5 2.7 %collective-permute-done.3.refs_3_ = bf16[4,256,256]{2,1,0:T(8,128)(2,1)} collective-permute-done((bf16[4,256,256]{2,1,0:T(8,128)(2,1)}, bf16[4,256,256]{2,1,0:T(8,128)(2,1)}, u32[]{:S(2)}, u32[]{:S(2)}) %collective-permute-start.3) | collective-permute-done | bytes 524320 | tf_op jit(solution)/shard_map/ppermute | solution.py:192
  30.2 1.7 %collective-permute-done.4.refs_4_ = bf16[4,256,256]{2,1,0:T(8,128)(2,1)} collective-permute-done((bf16[4,256,256]{2,1,0:T(8,128)(2,1)S(1)}, bf16[4,256,256]{2,1,0:T(8,128)(2,1)}, u32[]{:S(2)}, u32[]{:S(2)}) %collective-permute-start.4) | collective-permute-done | bytes 524320 | tf_op jit(solution)/shard_map/ppermute | solution.py:193
  31.9 0.0 copy-done.8
  31.9 5.5 %cross_other.1 = bf16[4,288,256]{2,1,0:T(8,128)(2,1)} custom-call(s32[16]{0:T(128)S(1)} %reshape.7.ends, bf16[4,256,256]{2,1,0:T(8,128)(2,1)S(1)} %bitcast.4, bf16[4,256,256]{2,1,0:T(8,128)(2,1)S(1)} %collective-permute-done.refs_0_, bf16[4,256,256]{2,1,0:T(8,128)(2,1)S(1)} %collective-permute-done.1.refs_1_, ...), custom_call_target="tpu_custom_call" | custom-call | flops 805306368 | bytes 4194304 | tf_op jit(solution)/shard_map/cross_other/pallas_call | solution.py:207
  37.4 0.1 collective-permute-start.5
  37.5 0.0 copy-done.13
  37.5 0.6 %fusion = (s32[4,8,1]{1,2,0:T(1,128)}, s32[4,8]{1,0:T(4,128)S(1)}) fusion(s32[4,8,2]{1,2,0:T(2,128)S(1)} %copy-done.13), kind=kLoop, calls=%fused_computation.2 | loop fusion | bytes 512 | tf_op jit(solution)/shard_map/slice | solution.py:233
  38.1 0.6 %reshape_squeeze.3.peaks = s32[32]{0:T(128)} reshape(s32[4,8]{1,0:T(4,128)S(1)} %get-tuple-element.5) | data formatting | bytes 256 | tf_op jit(solution)/shard_map/reshape;squeeze | solution.py:233
  38.7 0.8 %copy.15.peak_columns = s32[4,8,1]{2,1,0:T(8,128)S(1)} copy(s32[4,8,1]{1,2,0:T(1,128)} %get-tuple-element.4) | data formatting | bytes 256
  39.4 0.0 copy-start.2
  39.4 1.0 %copy-done.2 = bf16[288,512]{1,0:T(8,128)(2,1)S(1)} copy-done((bf16[288,512]{1,0:T(8,128)(2,1)S(1)}, bf16[288,512]{1,0:T(8,128)(2,1)}, u32[]{:S(2)}) %copy-start.2) | copy-done | bytes 294936
  40.4 0.0 copy-start.5
  40.4 0.9 %copy-done.5 = bf16[256,256]{1,0:T(8,128)(2,1)S(1)} copy-done((bf16[256,256]{1,0:T(8,128)(2,1)S(1)}, bf16[256,256]{1,0:T(8,128)(2,1)}, u32[]{:S(2)}) %copy-start.5) | copy-done | bytes 131096
  41.3 0.0 copy-start.7
  41.3 0.9 %copy-done.7 = bf16[256,256]{1,0:T(8,128)(2,1)S(1)} copy-done((bf16[256,256]{1,0:T(8,128)(2,1)S(1)}, bf16[256,256]{1,0:T(8,128)(2,1)}, u32[]{:S(2)}) %copy-start.7) | copy-done | bytes 131096
  42.2 0.0 copy-start.9
  42.2 0.6 %copy-done.9 = s32[16]{0:T(128)S(1)} copy-done((s32[16]{0:T(128)S(1)}, s32[16]{0:T(128)}, u32[]{:S(2)}) %copy-start.9) | copy-done | bytes 88
  42.9 0.0 copy-start.10
  42.9 0.0 copy-start.11
  42.9 0.0 copy-start.12
  42.9 4.6 %cross_mine.1.mine = bf16[4,288,256]{2,1,0:T(8,128)(2,1)S(1)} custom-call(s32[16]{0:T(128)S(1)} %copy-done.9, bf16[4,256,256]{2,1,0:T(8,128)(2,1)S(1)} %bitcast.5, bf16[4,256,256]{2,1,0:T(8,128)(2,1)S(1)} %collective-permute-done.refs_0_, bf16[4,256,256]{2,1,0:T(8,128)(2,1)S(1)} %collective-permute-done.1.refs_1_, ...), custom_call_target="tpu_custom_call" | custom-call | flops 805306368 | bytes 4194304 | tf_op jit(solution)/shard_map/cross_mine/pallas_call | solution.py:207
  47.5 0.0 collective-permute-done.5.other
  47.5 0.0 copy-done.10
  47.5 0.0 copy-done.11
  47.5 0.0 copy-done.12
  47.6 3.4 %surface.1 = (bf16[4,256,256]{2,1,0:T(8,128)(2,1)}, f32[4,8]{1,0:T(4,128)}) custom-call(s32[32]{0:T(128)S(1)} %copy-done.10, bf16[4,288,256]{2,1,0:T(8,128)(2,1)S(1)} %cross_mine.1.mine, bf16[4,288,256]{2,1,0:T(8,128)(2,1)} %collective-permute-done.5.other, s32[4,8,1]{2,1,0:T(8,128)S(1)} %copy.15.peak_columns, bf16[512,512]{1,0:T(8,128)(2,1)S(1)} %copy-done.11, ...), custom_call_target="tpu_custom_call" | custom-call | flops 805306368 | bytes 4194304 | tf_op jit(solution)/shard_map/surface/pallas_call | solution.py:221
Async XLA Ops:
  0.6 22.1 %copy-start.3 = (bf16[256,512]{1,0:T(8,128)(2,1)S(1)}, bf16[256,512]{1,0:T(8,128)(2,1)}, u32[]{:S(2)}) copy-start(bf16[256,512]{1,0:T(8,128)(2,1)} %constant.35.clone.columns.refs_8_) | copy-start | bytes 786436
  0.6 22.1 %copy-start = (bf16[4,1,256,256]{3,2,1,0:T(8,128)(2,1)S(1)}, bf16[4,1,256,256]{3,2,1,0:T(8,128)(2,1)}, u32[]{:S(2)}) copy-start(bf16[4,1,256,256]{3,2,1,0:T(8,128)(2,1)} %param.9) | copy-start | bytes 1572868
  0.7 21.9 %copy-start.14 = (s32[8,2]{0,1:T(2,128)S(1)}, s32[8,2]{0,1:T(2,128)}, u32[]{:S(2)}) copy-start(s32[8,2]{0,1:T(2,128)} %param.10) | copy-start | bytes 196
  0.7 10.4 %collective-permute-start = (bf16[4,256,256]{2,1,0:T(8,128)(2,1)}, bf16[4,256,256]{2,1,0:T(8,128)(2,1)S(1)}, u32[]{:S(2)}, u32[]{:S(2)}) collective-permute-start(bf16[4,256,256]{2,1,0:T(8,128)(2,1)} %bitcast.1), channel_id=1, source_target_pairs={{0,4},{1,3},{2,6},{3,1},{4,0},{5,7},{6,2},{7,5},{8,12},{9,11},{10,... | collective-permute-start | bytes 1572872 | tf_op jit(solution)/shard_map/ppermute | solution.py:189
  11.1 8.8 %collective-permute-start.2 = (bf16[4,256,256]{2,1,0:T(8,128)(2,1)S(1)}, bf16[4,256,256]{2,1,0:T(8,128)(2,1)S(1)}, u32[]{:S(2)}, u32[]{:S(2)}) collective-permute-start(bf16[4,256,256]{2,1,0:T(8,128)(2,1)S(1)} %collective-permute-done.refs_0_), channel_id=1, source_target_pairs={{0,8},{1,0},{2,10},{3,2},{4,5},{5,13},{6,7},{7,15},{8,16},{9,1},{1... | collective-permute-start | bytes 1572872 | tf_op jit(solution)/shard_map/ppermute | solution.py:190
  13.1 9.4 %collective-permute-start.1 = (bf16[4,256,256]{2,1,0:T(8,128)(2,1)}, bf16[4,256,256]{2,1,0:T(8,128)(2,1)S(1)}, u32[]{:S(2)}, u32[]{:S(2)}) collective-permute-start(bf16[4,256,256]{2,1,0:T(8,128)(2,1)} %bitcast.2), channel_id=1, source_target_pairs={{0,2},{1,5},{2,0},{3,7},{4,6},{5,1},{6,4},{7,3},{8,10},{9,13},{10,... | collective-permute-start | bytes 1572872 | tf_op jit(solution)/shard_map/ppermute | solution.py:191
  20.7 9.5 %collective-permute-start.3 = (bf16[4,256,256]{2,1,0:T(8,128)(2,1)}, bf16[4,256,256]{2,1,0:T(8,128)(2,1)}, u32[]{:S(2)}, u32[]{:S(2)}) collective-permute-start(bf16[4,256,256]{2,1,0:T(8,128)(2,1)} %broadcast_select_fusion), channel_id=1, source_target_pairs={{0,2},{1,5},{2,0},{3,7},{4,6},{5,1},{6,4},{7,3},{8,10},{9,13},{10,... | collective-permute-start | bytes 1572872 | tf_op jit(solution)/shard_map/ppermute | solution.py:192
  22.5 9.4 %collective-permute-start.4 = (bf16[4,256,256]{2,1,0:T(8,128)(2,1)S(1)}, bf16[4,256,256]{2,1,0:T(8,128)(2,1)}, u32[]{:S(2)}, u32[]{:S(2)}) collective-permute-start(bf16[4,256,256]{2,1,0:T(8,128)(2,1)S(1)} %collective-permute-done.1.refs_1_), channel_id=1, source_target_pairs={{0,1},{1,9},{2,3},{3,11},{4,12},{5,4},{6,14},{7,6},{8,0},{9,17},{1... | collective-permute-start | bytes 1572872 | tf_op jit(solution)/shard_map/ppermute | solution.py:193
  22.7 1.0 %copy-start.1 = (bf16[288,512]{1,0:T(8,128)(2,1)S(1)}, bf16[288,512]{1,0:T(8,128)(2,1)}, u32[]{:S(2)}) copy-start(bf16[288,512]{1,0:T(8,128)(2,1)} %constant.36.clone.rows.refs_9_) | copy-start | bytes 884740
  23.7 0.9 %copy-start.4 = (bf16[256,256]{1,0:T(8,128)(2,1)S(1)}, bf16[256,256]{1,0:T(8,128)(2,1)}, u32[]{:S(2)}) copy-start(bf16[256,256]{1,0:T(8,128)(2,1)} %constant.33.clone.gauss_t.refs_6_) | copy-start | bytes 393220
  24.6 0.9 %copy-start.6 = (bf16[256,256]{1,0:T(8,128)(2,1)S(1)}, bf16[256,256]{1,0:T(8,128)(2,1)}, u32[]{:S(2)}) copy-start(bf16[256,256]{1,0:T(8,128)(2,1)} %constant.34.clone.gauss.refs_7_) | copy-start | bytes 393220
  25.5 6.4 %copy-start.8 = (s32[16]{0:T(128)}, s32[16]{0:T(128)S(1)}, u32[]{:S(2)}) copy-start(s32[16]{0:T(128)S(1)} %reshape.7.ends) | copy-start | bytes 196
  27.5 10.0 %copy-start.13 = (s32[4,8,2]{1,2,0:T(2,128)S(1)}, s32[4,8,2]{1,2,0:T(2,128)}, u32[]{:S(2)}) copy-start(s32[4,8,2]{1,2,0:T(2,128)} %param.11) | copy-start | bytes 772
  37.4 10.1 %collective-permute-start.5 = (bf16[4,288,256]{2,1,0:T(8,128)(2,1)}, bf16[4,288,256]{2,1,0:T(8,128)(2,1)}, u32[]{:S(2)}, u32[]{:S(2)}) collective-permute-start(bf16[4,288,256]{2,1,0:T(8,128)(2,1)} %cross_other.1), channel_id=1, source_target_pairs={{0,1},{1,0},{2,3},{3,2},{4,5},{5,4},{6,7},{7,6},{8,9},{9,8},{10,11... | collective-permute-start | bytes 1769480 | tf_op jit(solution)/shard_map/ppermute | solution.py:219
  39.4 1.0 %copy-start.2 = (bf16[288,512]{1,0:T(8,128)(2,1)S(1)}, bf16[288,512]{1,0:T(8,128)(2,1)}, u32[]{:S(2)}) copy-start(bf16[288,512]{1,0:T(8,128)(2,1)} %constant.36.clone.rows.refs_9_) | copy-start | bytes 884740
  40.4 0.9 %copy-start.5 = (bf16[256,256]{1,0:T(8,128)(2,1)S(1)}, bf16[256,256]{1,0:T(8,128)(2,1)}, u32[]{:S(2)}) copy-start(bf16[256,256]{1,0:T(8,128)(2,1)} %constant.33.clone.gauss_t.refs_6_) | copy-start | bytes 393220
  41.3 0.9 %copy-start.7 = (bf16[256,256]{1,0:T(8,128)(2,1)S(1)}, bf16[256,256]{1,0:T(8,128)(2,1)}, u32[]{:S(2)}) copy-start(bf16[256,256]{1,0:T(8,128)(2,1)} %constant.34.clone.gauss.refs_7_) | copy-start | bytes 393220
  42.2 0.6 %copy-start.9 = (s32[16]{0:T(128)S(1)}, s32[16]{0:T(128)}, u32[]{:S(2)}) copy-start(s32[16]{0:T(128)} %copy-done.8) | copy-start | bytes 196
  42.9 4.7 %copy-start.10 = (s32[32]{0:T(128)S(1)}, s32[32]{0:T(128)}, u32[]{:S(2)}) copy-start(s32[32]{0:T(128)} %reshape_squeeze.3.peaks) | copy-start | bytes 388
  42.9 4.7 %copy-start.11 = (bf16[512,512]{1,0:T(8,128)(2,1)S(1)}, bf16[512,512]{1,0:T(8,128)(2,1)}, u32[]{:S(2)}) copy-start(bf16[512,512]{1,0:T(8,128)(2,1)} %constant.37.clone.back) | copy-start | bytes 1572868
  42.9 4.7 %copy-start.12 = (bf16[256,256]{1,0:T(8,128)(2,1)S(1)}, bf16[256,256]{1,0:T(8,128)(2,1)}, u32[]{:S(2)}) copy-start(bf16[256,256]{1,0:T(8,128)(2,1)} %constant.38.clone.last) | copy-start | bytes 393220

commit v2 on v1

v2 whole, which is shorter than its diff:
```python
import functools
import math

import jax
import jax.numpy as jnp
import ml_dtypes
import numpy as np
from jax import lax
from jax.experimental import pallas as pl
from jax.experimental.pallas import tpu as pltpu
from jax.sharding import PartitionSpec as P

SIGMA = 0.5
FLOOR = 0.05
PLANE = 4
EXTRA = 16
BOTH = ("tile", "chan")
VMEM = pl.BlockSpec(memory_space=pltpu.VMEM)
SMEM = pl.BlockSpec(memory_space=pltpu.SMEM)


def tables(size):
    index = np.arange(size)
    angle = (index[:, None] * index[None, :] % size) * (2.0 * math.pi / size)
    cosine = np.cos(angle).astype(ml_dtypes.bfloat16).astype(np.float64)
    sine = np.sin(angle).astype(ml_dtypes.bfloat16).astype(np.float64)
    offset = index[:, None] - index[None, :]
    weight = np.exp(-offset * offset / (2.0 * SIGMA * SIGMA))
    gauss = weight / weight.sum(axis=1, keepdims=True)
    half = size // 2
    columns = np.concatenate([cosine, -sine], axis=1)
    pad = np.zeros((EXTRA - 1, 2 * size))
    real = np.concatenate([cosine, sine], axis=1) / size
    imag = np.concatenate([-sine, cosine], axis=1) / size
    rows = np.concatenate([real[:half], imag[:half], real[half : half + 1], pad, imag[half : half + 1], pad], axis=0)
    back = np.block([[cosine, sine], [-sine, cosine]])
    twice = np.full((1, half), 2.0)
    twice[0, 0] = 1.0
    sines = -sine[:, :half] * twice
    sines[:, 0] = cosine[:, half]
    last = np.concatenate([cosine[:, :half] * twice, sines], axis=1) / size
    wide = np.concatenate([gauss.T, gauss], axis=1)
    narrow = np.concatenate([last, np.zeros((size, size))], axis=1)
    return jnp.asarray(np.concatenate([wide, columns, back, narrow, rows], axis=0).astype(ml_dtypes.bfloat16))


def product(left, right):
    return jnp.dot(left, right, preferred_element_type=jnp.float32)


def spectra_of(panels, table):
    count, size, _ = panels.shape
    first = product(panels.reshape(count * size, size), table[:size, :size]).astype(jnp.bfloat16)
    gauss = table[:size, size:]
    smooth = [product(gauss, first[k * size : (k + 1) * size]).astype(jnp.bfloat16) for k in range(count)]
    part = product(jnp.concatenate(smooth, axis=0), table[size : 2 * size]).astype(jnp.bfloat16)
    rows = table[5 * size :]
    slabs = []
    for k in range(count):
        one = part[k * size : (k + 1) * size]
        slabs.append(product(rows, jnp.concatenate([one[:, :size], one[:, size:]], axis=0)))
    return slabs


def local_kernel(panels, table, out):
    for k, slab in enumerate(spectra_of(panels[...], table)):
        out[k] = slab


def split(slab, half):
    return (slab[:half], slab[half : 2 * half], slab[2 * half : 2 * half + EXTRA], slab[2 * half + EXTRA :])


def cross_kernel(mine, ends, panels, *refs):
    blocks, (spectra, table, out, taken) = refs[:5], refs[5:]
    here = lax.axis_index("tile")
    chan = lax.axis_index("chan")
    tile_dev = panels.shape[0]
    half = panels.shape[-1] // 2
    count = out.shape[0]
    first_pair = count * (chan if mine else 1 - chan)
    place = here % PLANE
    one = jnp.where(place % 2 == 0, 1, -1)
    two = jnp.where(place < 2, 2, -2)
    even = chan == 0
    held = (0, jnp.where(even, two, one), jnp.where(even, one, two), jnp.where(even, -two, 0), -one, jnp.where(even, 0, -two))
    for k in range(count):
        tile = ends[2 * (first_pair + k) + 1]
        away = tile // tile_dev - here
        slot = tile % tile_dev
        for index, (distance, source) in enumerate(zip(held, (panels, *blocks))):

            @pl.when(away == distance if index in (0, 1, 2, 4) else (away == distance) & (distance != 0))
            def _(source=source):
                taken[k] = source[slot]

    for k, slab in enumerate(spectra_of(taken[...], table)):
        b_real, b_imag, b_real_x, b_imag_x = split(slab, half)
        a = spectra.at[ends[2 * (first_pair + k)] - here * tile_dev]
        a_real, a_imag, a_real_x, a_imag_x = split(a[...], half)
        out[k] = jnp.concatenate(
            [
                a_real * b_real + a_imag * b_imag,
                a_imag * b_real - a_real * b_imag,
                a_real_x * b_real_x + a_imag_x * b_imag_x,
                a_imag_x * b_real_x - a_real_x * b_imag_x,
            ],
            axis=0,
        ).astype(jnp.bfloat16)


def surface_kernel(peaks, mine, other, peak_columns, table, surface, scores, corr):
    count, _, size = surface.shape
    cand = scores.shape[1]
    half = size // 2
    parts = []
    for k in range(count):
        slab = mine[k].astype(jnp.float32) + other[k].astype(jnp.float32)
        real, imag, real_x, imag_x = split(slab, half)
        magnitude = jnp.sqrt(real * real + imag * imag)
        magnitude_x = jnp.sqrt(real_x * real_x + imag_x * imag_x)
        total = 2.0 * jnp.sum(magnitude) - jnp.sum(magnitude[:1]) + jnp.sum(magnitude_x)
        level = total / (size * size) + 1e-06
        scale = 1.0 / (magnitude + FLOOR * level)
        scale_x = 1.0 / (magnitude_x + FLOOR * level)
        q_real = jnp.concatenate([real * scale, real_x * scale_x], axis=0)
        q_imag = jnp.concatenate([imag * scale, imag_x * scale_x], axis=0)
        parts.append(jnp.concatenate([q_real, q_imag], axis=1).astype(jnp.bfloat16))
    spread = half + EXTRA
    y_all = product(jnp.concatenate(parts, axis=0), table[2 * size : 4 * size])
    last = table[4 * size : 5 * size, :size]
    for k in range(count):
        y = y_all[k * spread : (k + 1) * spread]
        y_real = y[:half, :size]
        y_imag = y[:half, size:]
        row = lax.broadcasted_iota(jnp.int32, y_imag.shape, 0)
        y_imag = jnp.where(row == 0, y[half : half + 1, :size], y_imag)
        both = jnp.concatenate([y_real, y_imag], axis=0).astype(jnp.bfloat16)
        result = product(last, both)
        corr[k] = result
        surface[k] = result.astype(jnp.bfloat16)
    lane = lax.broadcasted_iota(jnp.int32, (cand, size), 1)
    diagonal = lax.broadcasted_iota(jnp.int32, (cand, cand), 0) == lax.broadcasted_iota(jnp.int32, (cand, cand), 1)
    for k in range(count):
        picked = jnp.concatenate([corr[k, pl.ds(peaks[k * cand + j], 1), :] for j in range(cand)], axis=0)
        found = jnp.sum(jnp.where(lane == peak_columns[k], picked, 0.0), axis=1, keepdims=True)
        scores[k : k + 1, :] = jnp.sum(jnp.where(diagonal, found, 0.0), axis=0, keepdims=True)


def routes(devices):
    def up(t, c):
        return (t + PLANE, c) if t + PLANE < devices else (t, 1 - c)

    def down(t, c):
        return (t - PLANE, c) if t >= PLANE else (t, 1 - c)

    def across(c, core):
        return 2 if c == core else 1

    def pairs(step):
        return [(2 * t + c, 2 * d + e) for t in range(devices) for c in range(2) for d, e in [step(t, c)]]

    return (
        pairs(lambda t, c: (t ^ across(c, 0), c)),
        pairs(lambda t, c: (t ^ across(c, 1), c)),
        pairs(lambda t, c: (up if (t % PLANE < 2) == (c == 0) else down)(t, c)),
        pairs(lambda t, c: (t ^ across(c, 1), c)),
        pairs(lambda t, c: (up if (t % PLANE < 2) == (c == 1) else down)(t, c)),
    )


def after(value, *earlier):
    return lax.optimization_barrier((value, *earlier))[0]


def call(kernel, name, operands, scalars, out, scratch=()):
    return pl.pallas_call(
        kernel,
        out_shape=out,
        in_specs=[SMEM] * scalars + [VMEM] * (len(operands) - scalars),
        out_specs=jax.tree.map(lambda _: VMEM, out),
        scratch_shapes=scratch,
        compiler_params=pltpu.CompilerParams(vmem_limit_bytes=16 << 20),
        cost_estimate=pl.CostEstimate(flops=1 << 30, bytes_accessed=4 << 20, transcendentals=0),
        name=name,
    )(*operands)


def shards(panels, pair_ends, peaks):
    tile_dev, _, size, _ = panels.shape
    share, cand, _ = peaks.shape
    devices = lax.axis_size("tile")
    local = panels[:, 0]
    table = tables(size)
    slab = size + 2 * EXTRA
    place = lax.axis_index("tile") % PLANE
    outer = (place == 0) | (place == 3)
    swap, cross_swap, climb, relay, climb_late = routes(devices)
    move = functools.partial(lax.ppermute, axis_name=BOTH)
    ends = pair_ends.reshape(-1)
    peak_rows = peaks[:, :, 0].reshape(-1)
    peak_columns = peaks[:, :, 1:]
    got_swap = move(local, perm=swap)
    spectra = call(local_kernel, "local_spectra", (local, table), 0, jax.ShapeDtypeStruct((tile_dev, slab, size), jnp.float32))
    got_climb = move(got_swap, perm=climb)
    got_cross = move(after(local, spectra, ends, peak_rows, peak_columns), perm=cross_swap)
    got_relay = move(jnp.where(outer, got_swap, got_climb), perm=relay)
    got_late = move(got_cross, perm=climb_late)
    blocks = (got_swap, got_cross, got_climb, got_relay, got_late)

    def cross(mine):
        return call(
            functools.partial(cross_kernel, mine),
            "cross_mine" if mine else "cross_other",
            (ends, local, *blocks, spectra, table),
            1,
            jax.ShapeDtypeStruct((share, slab, size), jnp.bfloat16),
            [pltpu.VMEM((share, size, size), jnp.bfloat16)],
        )

    given = cross(False)
    other = lax.ppermute(given, "chan", [(0, 1), (1, 0)])
    kept = cross(True)
    surface, scores = call(
        surface_kernel,
        "surface",
        (peak_rows, kept, other, peak_columns, table),
        1,
        (jax.ShapeDtypeStruct((share, size, size), jnp.bfloat16), jax.ShapeDtypeStruct((share, cand), jnp.float32)),
        [pltpu.VMEM((share, size, size), jnp.float32)],
    )
    return (surface, scores)


def solution(mesh):
    in_specs = (P("tile", "chan", None, None), P("tile", None), P(BOTH, None, None))
    out_specs = (P(BOTH, None, None), P(BOTH, None))
    return jax.shard_map(shards, mesh=mesh, in_specs=in_specs, out_specs=out_specs, check_vma=False)
```

time: 51.4 us -> 41.1 us (0.80)
  the two profiles are of different devices: /device:TPU:0 before, /device:TPU:19 now
where the time goes in v2:
time: 41.1 us; the launch traced here: 40.8 us
  waiting for transfers between devices  16.6 us (40%)
  Pallas kernels  10.2 us (25%)
  starting transfers between devices  8.94 us (22%)
  local copies, waits for them, and re-layouts  3.23 us (8%)
  other arithmetic  1.1 us (3%)
  between operations  0.68 us (2%)
    pallas_call x4, Pallas kernels, call(): pl.pallas_call(kernel, out_shape=out, in_specs=[SMEM] * scalars + [VMEM]...  10.2 us
    ppermute x1, waiting for transfers between devices, shards(): got_late = move(got_cross, perm=climb_late)  7.04 us
    ppermute x1, waiting for transfers between devices, shards(): move(after(local, spectra, ends, peak_rows, peak_columns), perm=cross_swap)  6.69 us
    ppermute x1, starting transfers between devices, shards(): other = lax.ppermute(given, 'chan', [(0, 1), (1, 0)])  5.59 us
    unnamed x6, local copies, waits for them, and re-layouts  2.28 us
    ppermute x1, waiting for transfers between devices, shards(): got_swap = move(local, perm=swap)  1.51 us
    ppermute x1, starting transfers between devices, shards(): move(after(local, spectra, ends, peak_rows, peak_columns), perm=cross_swap)  1.31 us
    ppermute x1, starting transfers between devices, shards(): got_late = move(got_cross, perm=climb_late)  1.3 us
  transfers between devices with their start and end apart: 6, of which 5 were waited for; matrix products, arithmetic and copies ran while one was open for 7% of the time, Pallas kernels for 12%

profile of v2, /device:TPU:19, one launch (start us, length us, event | category | flops | bytes accessed | tf_op | source)
XLA Modules:
  0.0 40.8 jit_solution(12101959046311776900)
XLA Ops:
  0.6 0.3 collective-permute-start
  0.9 0.8 %copy.8 = s32[8,2]{1,0:T(8,128)S(1)} copy(s32[8,2]{0,1:T(2,128)} %param.5) | data formatting | bytes 128 | tf_op args[1]
  1.7 0.1 reshape.7.ends
  1.8 0.8 %fusion = (s32[4,8,1]{1,2,0:T(1,128)S(1)}, s32[4,8]{1,0:T(4,128)S(1)}) fusion(s32[4,8,2]{1,2,0:T(2,128)} %param.6), kind=kLoop, calls=%fused_computation.2 | loop fusion | bytes 512 | tf_op jit(solution)/shard_map/slice | solution.py:202
  2.6 0.1 reshape_squeeze.3.peaks
  2.7 0.1 copy.10.peak_columns
  2.8 0.0 copy-start
  2.8 1.4 %copy-done = bf16[1568,512]{1,0:T(8,128)(2,1)S(1)} copy-done((bf16[1568,512]{1,0:T(8,128)(2,1)S(1)}, bf16[1568,512]{1,0:T(8,128)(2,1)}, u32[]{:S(2)}) %copy-start) | copy-done | bytes 1605656
  4.2 2.2 %local_spectra.1.refs_5_ = f32[4,288,256]{2,1,0:T(8,128)S(1)} custom-call(bf16[4,256,256]{2,1,0:T(8,128)(2,1)} %bitcast.panels, bf16[1568,512]{1,0:T(8,128)(2,1)S(1)} %copy-done), custom_call_target="tpu_custom_call" | custom-call | flops 1073741824 | bytes 4194304 | tf_op jit(solution)/shard_map/local_spectra/pallas_call | solution.py:177
  6.4 0.0 copy-start.1
  6.4 1.3 %collective-permute-start.1 = (bf16[4,256,256]{2,1,0:T(8,128)(2,1)}, bf16[4,256,256]{2,1,0:T(8,128)(2,1)}, u32[]{:S(2)}, u32[]{:S(2)}) collective-permute-start(bf16[4,256,256]{2,1,0:T(8,128)(2,1)} %bitcast.panels), channel_id=1, source_target_pairs={{0,2},{1,5},{2,0},{3,7},{4,6},{5,1},{6,4},{7,3},{8,10},{9,13},{10,... | collective-permute-start | bytes 1572872 | tf_op jit(solution)/shard_map/ppermute | solution.py:206
  7.7 1.5 %collective-permute-done.refs_0_ = bf16[4,256,256]{2,1,0:T(8,128)(2,1)S(1)} collective-permute-done((bf16[4,256,256]{2,1,0:T(8,128)(2,1)}, bf16[4,256,256]{2,1,0:T(8,128)(2,1)S(1)}, u32[]{:S(2)}, u32[]{:S(2)}) %collective-permute-start) | collective-permute-done | bytes 524320 | tf_op jit(solution)/shard_map/ppermute | solution.py:203
  9.2 0.2 collective-permute-start.2
  9.4 6.7 %collective-permute-done.1.refs_1_ = bf16[4,256,256]{2,1,0:T(8,128)(2,1)} collective-permute-done((bf16[4,256,256]{2,1,0:T(8,128)(2,1)}, bf16[4,256,256]{2,1,0:T(8,128)(2,1)}, u32[]{:S(2)}, u32[]{:S(2)}) %collective-permute-start.1) | collective-permute-done | bytes 524320 | tf_op jit(solution)/shard_map/ppermute | solution.py:206
  16.1 1.3 %collective-permute-start.4 = (bf16[4,256,256]{2,1,0:T(8,128)(2,1)}, bf16[4,256,256]{2,1,0:T(8,128)(2,1)S(1)}, u32[]{:S(2)}, u32[]{:S(2)}) collective-permute-start(bf16[4,256,256]{2,1,0:T(8,128)(2,1)} %collective-permute-done.1.refs_1_), channel_id=1, source_target_pairs={{0,1},{1,9},{2,3},{3,11},{4,12},{5,4},{6,14},{7,6},{8,0},{9,17},{1... | collective-permute-start | bytes 1572872 | tf_op jit(solution)/shard_map/ppermute | solution.py:208
  17.4 0.3 collective-permute-done.2.refs_2_
  17.7 1.1 %broadcast_select_fusion = bf16[4,256,256]{2,1,0:T(8,128)(2,1)S(1)} fusion(bf16[4,256,256]{2,1,0:T(8,128)(2,1)S(1)} %collective-permute-done.refs_0_, bf16[4,256,256]{2,1,0:T(8,128)(2,1)} %collective-permute-done.2.refs_2_, pred[]{:T(512)S(6)} %or.3), kind=kLoop, calls=%fused_computation | loop fusion | flops 262144 | bytes 1572865 | tf_op jit(solution)/shard_map/jit(_where)/select_n | solution.py:207
  18.8 0.3 collective-permute-start.3
  19.0 7.0 %collective-permute-done.4.refs_4_ = bf16[4,256,256]{2,1,0:T(8,128)(2,1)S(1)} collective-permute-done((bf16[4,256,256]{2,1,0:T(8,128)(2,1)}, bf16[4,256,256]{2,1,0:T(8,128)(2,1)S(1)}, u32[]{:S(2)}, u32[]{:S(2)}) %collective-permute-start.4) | collective-permute-done | bytes 524320 | tf_op jit(solution)/shard_map/ppermute | solution.py:208
  26.1 1.1 %collective-permute-done.3.refs_3_ = bf16[4,256,256]{2,1,0:T(8,128)(2,1)S(1)} collective-permute-done((bf16[4,256,256]{2,1,0:T(8,128)(2,1)S(1)}, bf16[4,256,256]{2,1,0:T(8,128)(2,1)S(1)}, u32[]{:S(2)}, u32[]{:S(2)}) %collective-permute-start.3) | collective-permute-done | bytes 524320 | tf_op jit(solution)/shard_map/ppermute | solution.py:207
  27.2 0.0 copy-done.1
  27.2 2.8 %cross_other.1 = bf16[4,288,256]{2,1,0:T(8,128)(2,1)S(1)} custom-call(s32[16]{0:T(128)S(1)} %reshape.7.ends, bf16[4,256,256]{2,1,0:T(8,128)(2,1)} %bitcast.panels, bf16[4,256,256]{2,1,0:T(8,128)(2,1)S(1)} %collective-permute-done.refs_0_, bf16[4,256,256]{2,1,0:T(8,128)(2,1)} %collective-permute-done.1.refs_1_, ...), custom_call_target="tpu_custom_call" | custom-call | flops 1073741824 | bytes 4194304 | tf_op jit(solution)/shard_map/cross_other/pallas_call | solution.py:177
  30.0 5.6 %collective-permute-start.5 = (bf16[4,288,256]{2,1,0:T(8,128)(2,1)S(1)}, bf16[4,288,256]{2,1,0:T(8,128)(2,1)S(1)}, u32[]{:S(2)}, u32[]{:S(2)}) collective-permute-start(bf16[4,288,256]{2,1,0:T(8,128)(2,1)S(1)} %cross_other.1), channel_id=1, source_target_pairs={{0,1},{1,0},{2,3},{3,2},{4,5},{5,4},{6,7},{7,6},{8,9},{9,8},{10,11... | collective-permute-start | bytes 1769480 | tf_op jit(solution)/shard_map/ppermute | solution.py:222
  35.5 2.8 %cross_mine.1.mine = bf16[4,288,256]{2,1,0:T(8,128)(2,1)S(1)} custom-call(s32[16]{0:T(128)S(1)} %reshape.7.ends, bf16[4,256,256]{2,1,0:T(8,128)(2,1)} %bitcast.panels, bf16[4,256,256]{2,1,0:T(8,128)(2,1)S(1)} %collective-permute-done.refs_0_, bf16[4,256,256]{2,1,0:T(8,128)(2,1)} %collective-permute-done.1.refs_1_, ...), custom_call_target="tpu_custom_call" | custom-call | flops 1073741824 | bytes 4194304 | tf_op jit(solution)/shard_map/cross_mine/pallas_call | solution.py:177
  38.3 0.0 collective-permute-done.5.other
  38.4 2.4 %surface.1 = (bf16[4,256,256]{2,1,0:T(8,128)(2,1)}, f32[4,8]{1,0:T(4,128)}) custom-call(s32[32]{0:T(128)S(1)} %reshape_squeeze.3.peaks, bf16[4,288,256]{2,1,0:T(8,128)(2,1)S(1)} %cross_mine.1.mine, bf16[4,288,256]{2,1,0:T(8,128)(2,1)S(1)} %collective-permute-done.5.other, s32[4,8,1]{2,1,0:T(8,128)S(1)} %copy.10.peak_columns, bf16[1568,512]{1,0:T(8,128)(2,1)S(1)} %copy-done.1), custom_call_target="tpu_custom_call" | custom-call | flops 1073741824 | bytes 4194304 | tf_op jit(solution)/shard_map/surface/pallas_call | solution.py:177
Async XLA Ops:
  0.6 8.6 %collective-permute-start = (bf16[4,256,256]{2,1,0:T(8,128)(2,1)}, bf16[4,256,256]{2,1,0:T(8,128)(2,1)S(1)}, u32[]{:S(2)}, u32[]{:S(2)}) collective-permute-start(bf16[4,256,256]{2,1,0:T(8,128)(2,1)} %bitcast.panels), channel_id=1, source_target_pairs={{0,4},{1,3},{2,6},{3,1},{4,0},{5,7},{6,2},{7,5},{8,12},{9,11},{10,... | collective-permute-start | bytes 1572872 | tf_op jit(solution)/shard_map/ppermute | solution.py:203
  2.8 1.4 %copy-start = (bf16[1568,512]{1,0:T(8,128)(2,1)S(1)}, bf16[1568,512]{1,0:T(8,128)(2,1)}, u32[]{:S(2)}) copy-start(bf16[1568,512]{1,0:T(8,128)(2,1)} %constant.23.clone.table.refs_6_) | copy-start | bytes 4816900
  6.4 20.8 %copy-start.1 = (bf16[1568,512]{1,0:T(8,128)(2,1)S(1)}, bf16[1568,512]{1,0:T(8,128)(2,1)}, u32[]{:S(2)}) copy-start(bf16[1568,512]{1,0:T(8,128)(2,1)} %constant.23.clone.table.refs_6_) | copy-start | bytes 4816900
  6.4 9.7 %collective-permute-start.1 = (bf16[4,256,256]{2,1,0:T(8,128)(2,1)}, bf16[4,256,256]{2,1,0:T(8,128)(2,1)}, u32[]{:S(2)}, u32[]{:S(2)}) collective-permute-start(bf16[4,256,256]{2,1,0:T(8,128)(2,1)} %bitcast.panels), channel_id=1, source_target_pairs={{0,2},{1,5},{2,0},{3,7},{4,6},{5,1},{6,4},{7,3},{8,10},{9,13},{10,... | collective-permute-start | bytes 1572872 | tf_op jit(solution)/shard_map/ppermute | solution.py:206
  9.2 8.4 %collective-permute-start.2 = (bf16[4,256,256]{2,1,0:T(8,128)(2,1)S(1)}, bf16[4,256,256]{2,1,0:T(8,128)(2,1)}, u32[]{:S(2)}, u32[]{:S(2)}) collective-permute-start(bf16[4,256,256]{2,1,0:T(8,128)(2,1)S(1)} %collective-permute-done.refs_0_), channel_id=1, source_target_pairs={{0,8},{1,0},{2,10},{3,2},{4,5},{5,13},{6,7},{7,15},{8,16},{9,1},{1... | collective-permute-start | bytes 1572872 | tf_op jit(solution)/shard_map/ppermute | solution.py:205
  16.1 10.0 %collective-permute-start.4 = (bf16[4,256,256]{2,1,0:T(8,128)(2,1)}, bf16[4,256,256]{2,1,0:T(8,128)(2,1)S(1)}, u32[]{:S(2)}, u32[]{:S(2)}) collective-permute-start(bf16[4,256,256]{2,1,0:T(8,128)(2,1)} %collective-permute-done.1.refs_1_), channel_id=1, source_target_pairs={{0,1},{1,9},{2,3},{3,11},{4,12},{5,4},{6,14},{7,6},{8,0},{9,17},{1... | collective-permute-start | bytes 1572872 | tf_op jit(solution)/shard_map/ppermute | solution.py:208
  18.8 8.4 %collective-permute-start.3 = (bf16[4,256,256]{2,1,0:T(8,128)(2,1)S(1)}, bf16[4,256,256]{2,1,0:T(8,128)(2,1)S(1)}, u32[]{:S(2)}, u32[]{:S(2)}) collective-permute-start(bf16[4,256,256]{2,1,0:T(8,128)(2,1)S(1)} %broadcast_select_fusion), channel_id=1, source_target_pairs={{0,2},{1,5},{2,0},{3,7},{4,6},{5,1},{6,4},{7,3},{8,10},{9,13},{10,... | collective-permute-start | bytes 1572872 | tf_op jit(solution)/shard_map/ppermute | solution.py:207
  30.0 8.4 %collective-permute-start.5 = (bf16[4,288,256]{2,1,0:T(8,128)(2,1)S(1)}, bf16[4,288,256]{2,1,0:T(8,128)(2,1)S(1)}, u32[]{:S(2)}, u32[]{:S(2)}) collective-permute-start(bf16[4,288,256]{2,1,0:T(8,128)(2,1)S(1)} %cross_other.1), channel_id=1, source_target_pairs={{0,1},{1,0},{2,3},{3,2},{4,5},{5,4},{6,7},{7,6},{8,9},{9,8},{10,11... | collective-permute-start | bytes 1769480 | tf_op jit(solution)/shard_map/ppermute | solution.py:222
